TPU v7x, 32 devices: a whole 2x2x4 slice. The times are simulated.
32 devices in a mesh: ga: 4 (over z), orb: 8 (over y, x, core).
Axes of the slice: x: 2, y: 2, z: 4, core: 2. Of those that a mesh axis runs over, the one named last changes fastest.
Arguments:
- coefficients: bfloat16 [2, 294912, 512], P(None, ('ga', 'orb')), may hold values from -0.01171875 to 0.01171875
- triples: int32 [3, 294912], P(None, ('ga', 'orb')), may hold values from -33 to 33
- elec_pos: float32 [3, 32], P(None, ('ga', 'orb')), may hold values from 0 to 1
- ion_pos: float32 [3, 128], replicated, may hold values from 0 to 1
- assignment: int32 [32], P(('ga', 'orb')), may hold values from 0 to 127
- rotation: int32 [32], P(('ga', 'orb')), may hold values from 0 to 63
- quad_table: float32 [64, 3, 12], replicated, may hold values from -2.4 to 2.4
- inverse_rows: float32 [32, 512], P(('ga', 'orb')), may hold values from -0.25 to 0.25
Outputs:
- ratios: float32 [32, 12], P(('ga', 'orb'))
All inputs are finite; a program needn't handle non-finite values.
Results may differ from a plain program's by a relative error of at most 0.0024.
Values may be sent and summed in bfloat16 or wider, within the bound.
A program may use at most 64 MiB of HBM per device.

v0:
```python
import math

import jax
import jax.numpy as jnp
from jax import lax
from jax.sharding import PartitionSpec as P

TWO_PI = 2.0 * math.pi


def point_coords(elec_pos, ion_pos, assignment, rotation, quad_table):
    ion_rows = jnp.take(ion_pos, assignment, axis=1)
    offsets = elec_pos - ion_rows
    radius = jnp.sqrt(jnp.sum(offsets * offsets, axis=0))
    displace = jnp.take(quad_table, rotation, axis=0)
    located = ion_rows.T[:, :, None] + radius[:, None, None] * displace
    return jnp.transpose(located, (1, 0, 2)).reshape(3, -1)


def phase_values(points, triples, coefficients):
    point_count = points.shape[1]
    wave_count = triples.shape[1]
    columns = coefficients.shape[2]
    block_rows = math.gcd(point_count, 512)
    span_cols = wave_count if wave_count <= 4096 else math.gcd(wave_count, 4096)
    waves = triples.astype(jnp.float32) * TWO_PI

    def one_block(block_points):

        def add_panel(step_index, running):
            offset = step_index * span_cols
            wave_part = lax.dynamic_slice_in_dim(waves, offset, span_cols, 1)
            angle = (
                block_points[0][:, None] * wave_part[0][None, :]
                + block_points[1][:, None] * wave_part[1][None, :]
                + block_points[2][:, None] * wave_part[2][None, :]
            )
            phases = jnp.concatenate(
                [jnp.cos(angle).astype(jnp.bfloat16), jnp.sin(angle).astype(jnp.bfloat16)], axis=1
            )
            weights = lax.dynamic_slice_in_dim(coefficients, offset, span_cols, 1).reshape(
                2 * span_cols, columns
            )
            return running + jnp.dot(phases, weights, preferred_element_type=jnp.float32)

        initial = jnp.zeros((block_rows, columns), jnp.float32)
        return lax.fori_loop(0, wave_count // span_cols, add_panel, initial)

    blocks = jnp.transpose(points.reshape(3, point_count // block_rows, block_rows), (1, 0, 2))
    return lax.map(one_block, blocks).reshape(point_count, columns)


def on_device(
    coefficients, triples, elec_pos, ion_pos, assignment, rotation, quad_table, inverse_rows
):
    local_points = point_coords(elec_pos, ion_pos, assignment, rotation, quad_table)
    all_points = lax.all_gather(local_points, ("ga", "orb"), axis=1, tiled=True)
    group_count = lax.axis_size("ga")
    orbit_count = lax.axis_size("orb")
    own_rows = local_points.shape[1]
    electrons = inverse_rows.shape[0]
    total_rows = all_points.shape[1]
    reordered = jnp.transpose(
        all_points.reshape(3, group_count, orbit_count, own_rows), (0, 2, 1, 3)
    ).reshape(3, total_rows)
    group_values = lax.psum_scatter(
        phase_values(reordered, triples, coefficients), "orb", scatter_dimension=0, tiled=True
    )
    values = lax.psum_scatter(group_values, "ga", scatter_dimension=0, tiled=True)
    shaped = values.reshape(electrons, values.shape[0] // electrons, values.shape[1])
    return jnp.sum(shaped * inverse_rows[:, None, :], axis=2)


def solution(mesh):
    return jax.shard_map(
        on_device,
        mesh=mesh,
        in_specs=(
            P(None, ("ga", "orb"), None),
            P(None, ("ga", "orb")),
            P(None, ("ga", "orb")),
            P(),
            P(("ga", "orb")),
            P(("ga", "orb")),
            P(),
            P(("ga", "orb"), None),
        ),
        out_specs=P(("ga", "orb"), None),
        check_vma=False,
    )
```

profile of v0, /device:TPU:0, one launch (start us, length us, event | category | flops | bytes accessed | tf_op | source)
XLA Modules:
  0.0 237.5 jit_solution(9763473963645298922)
XLA Ops:
  7.9 1.4 fusion.8
  11.7 43.4 %all-gather = f32[32,12,3]{1,2,0:T(4,128)S(1)} all-gather(f32[1,12,3]{1,2,0:T(4,128)S(1)} %add_bitcast_fusion), channel_id=1, replica_groups=mesh['ga'=4,'orb'=8] {'ga','orb'}, dimensions={0}, use_global_device_ids=true | all-gather | bytes 4752 | tf_op jit(solution)/shard_map/all_gather | solution.py:57
  55.4 1.0 convert_multiply_fusion
  56.4 124.0 %while.27 = (s32[]{:T(128)}, f32[3,128,512]{2,1,0:T(8,128)}, f32[3,3,128]{2,0,1:T(4,128)S(1)}, f32[3,9216]{1,0:T(4,128)S(1)}, bf16[2,9216,512]{2,1,0:T(8,128)(2,...) while((s32[]{:T(128)}, f32[3,128,512]{2,1,0:T(8,128)}, ...), condition=%wide.region_4.5_spmd, body=%wide.region_1.0_spmd.sunk | while | flops 270532608 | bytes 8437166 | solution.py:50
  56.4 40.6 %while.28 = (s32[]{:T(128)}, f32[128,512]{1,0:T(8,128)S(1)}, f32[3,128]{1,0:T(4,128)S(1)}, f32[3,9216]{1,0:T(4,128)S(1)}, bf16[2,9216,512]{2,1,0:T(8,128)(2,1)},...) while((s32[]{:T(128)}, f32[128,512]{1,0:T(8,128)S(1)}, ...), condition=%wide.region_3.3_spmd.clone, body=%wide.region_2.2_spmd.clone.sunk | while | flops 270532608 | bytes 7905997 | solution.py:47
  56.6 2.2 cosine_convert_fusion.2
  58.7 1.7 constant_dynamic-slice_fusion.7
  61.1 2.2 cosine_convert_fusion.2
  63.2 1.7 constant_dynamic-slice_fusion.7
  65.6 2.2 cosine_convert_fusion.2
  67.7 1.7 constant_dynamic-slice_fusion.7
  70.1 2.2 cosine_convert_fusion.2
  72.3 1.7 constant_dynamic-slice_fusion.7
  74.6 2.2 cosine_convert_fusion.2
  76.8 1.7 constant_dynamic-slice_fusion.7
  79.1 2.2 cosine_convert_fusion.2
  81.3 1.7 constant_dynamic-slice_fusion.7
  83.6 2.2 cosine_convert_fusion.2
  85.8 1.7 constant_dynamic-slice_fusion.7
  88.1 2.2 cosine_convert_fusion.2
  90.3 1.7 constant_dynamic-slice_fusion.7
  92.6 2.2 cosine_convert_fusion.2
  94.8 1.7 constant_dynamic-slice_fusion.7
  97.8 40.6 %while.28 = (s32[]{:T(128)}, f32[128,512]{1,0:T(8,128)S(1)}, f32[3,128]{1,0:T(4,128)S(1)}, f32[3,9216]{1,0:T(4,128)S(1)}, bf16[2,9216,512]{2,1,0:T(8,128)(2,1)},...) while((s32[]{:T(128)}, f32[128,512]{1,0:T(8,128)S(1)}, ...), condition=%wide.region_3.3_spmd.clone, body=%wide.region_2.2_spmd.clone.sunk | while | flops 270532608 | bytes 7905997 | solution.py:47
  97.9 2.2 cosine_convert_fusion.2
  100.0 1.7 constant_dynamic-slice_fusion.7
  102.4 2.2 cosine_convert_fusion.2
  104.6 1.7 constant_dynamic-slice_fusion.7
  106.9 2.2 cosine_convert_fusion.2
  109.1 1.7 constant_dynamic-slice_fusion.7
  111.4 2.2 cosine_convert_fusion.2
  113.6 1.7 constant_dynamic-slice_fusion.7
  115.9 2.2 cosine_convert_fusion.2
  118.1 1.7 constant_dynamic-slice_fusion.7
  120.4 2.2 cosine_convert_fusion.2
  122.6 1.7 constant_dynamic-slice_fusion.7
  124.9 2.2 cosine_convert_fusion.2
  127.1 1.7 constant_dynamic-slice_fusion.7
  129.4 2.2 cosine_convert_fusion.2
  131.6 1.7 constant_dynamic-slice_fusion.7
  134.0 2.2 cosine_convert_fusion.2
  136.1 1.7 constant_dynamic-slice_fusion.7
  139.1 40.6 %while.28 = (s32[]{:T(128)}, f32[128,512]{1,0:T(8,128)S(1)}, f32[3,128]{1,0:T(4,128)S(1)}, f32[3,9216]{1,0:T(4,128)S(1)}, bf16[2,9216,512]{2,1,0:T(8,128)(2,1)},...) while((s32[]{:T(128)}, f32[128,512]{1,0:T(8,128)S(1)}, ...), condition=%wide.region_3.3_spmd.clone, body=%wide.region_2.2_spmd.clone.sunk | while | flops 270532608 | bytes 7905997 | solution.py:47
  139.2 2.2 cosine_convert_fusion.2
  141.4 1.7 constant_dynamic-slice_fusion.7
  143.7 2.2 cosine_convert_fusion.2
  145.9 1.7 constant_dynamic-slice_fusion.7
  148.2 2.2 cosine_convert_fusion.2
  150.4 1.7 constant_dynamic-slice_fusion.7
  152.7 2.2 cosine_convert_fusion.2
  154.9 1.7 constant_dynamic-slice_fusion.7
  157.2 2.2 cosine_convert_fusion.2
  159.4 1.7 constant_dynamic-slice_fusion.7
  161.7 2.2 cosine_convert_fusion.2
  163.9 1.7 constant_dynamic-slice_fusion.7
  166.3 2.2 cosine_convert_fusion.2
  168.4 1.7 constant_dynamic-slice_fusion.7
  170.8 2.2 cosine_convert_fusion.2
  172.9 1.7 constant_dynamic-slice_fusion.7
  175.3 2.2 cosine_convert_fusion.2
  177.4 1.7 constant_dynamic-slice_fusion.7
  180.4 31.3 %reduce-scatter.4.cloned.1.call-done = f32[48,512]{1,0:T(8,128)} async-done(((f32[384,512]{1,0:T(8,128)}), f32[48,512]{1,0:T(8,128)}) %reduce-scatter.4.cloned.1.call-update) | async-done | bytes 98320 | tf_op jit(solution)/shard_map/reduce_scatter | solution.py:66
  211.7 13.9 %fusion = f32[16,512]{1,0:T(8,128)S(1)} fusion(f32[48,512]{1,0:T(8,128)} %reduce-scatter.4.cloned.1.call-done), kind=kCustom, calls=%all-reduce-scatter | all-reduce-scatter fusion | flops 32769 | bytes 131584
  225.6 2.7 %collective-permute-start = (f32[12,512]{1,0:T(8,128)S(1)}, f32[12,512]{1,0:T(8,128)S(1)}, u32[]{:S(2)}, u32[]{:S(2)}) collective-permute-start(f32[12,512]{1,0:T(8,128)S(1)} %slice.64), channel_id=1, source_target_pairs={{0,8},{8,16},{16,24},{1,9},{9,17},{17,25},{2,10},{10,18},{18,26},{... | collective-permute-start | bytes 73736
  (113 shorter events, 21.1 us)
Async XLA Ops:
  6.5 205.1 %reduce-scatter.4.cloned.1.call-start = ((), (), s32[]{:S(2)}) async-start(), calls=%async_computation.1 | async-start | bytes 884736 | tf_op jit(solution)/shard_map/reduce_scatter | solution.py:66
  56.4 171.9 %copy-start.1 = (u32[32]{0:T(128)S(1)}, u32[32]{0:T(128)}, u32[]{:S(2)}) copy-start(u32[32]{0:T(128)} %constant.126) | copy-start | bytes 388
  56.4 173.6 %copy-start = (f32[1,512]{1,0:T(1,128)S(1)}, f32[1,512]{1,0:T(1,128)}, u32[]{:S(2)}) copy-start(f32[1,512]{1,0:T(1,128)} %param.19) | copy-start | bytes 6148
  225.6 4.3 %collective-permute-start = (f32[12,512]{1,0:T(8,128)S(1)}, f32[12,512]{1,0:T(8,128)S(1)}, u32[]{:S(2)}, u32[]{:S(2)}) collective-permute-start(f32[12,512]{1,0:T(8,128)S(1)} %slice.64), channel_id=1, source_target_pairs={{0,8},{8,16},{16,24},{1,9},{9,17},{17,25},{2,10},{10,18},{18,26},{... | collective-permute-start | bytes 73736
Sparse Core Ops, SparseCore 0:
  180.5 31.0 reduce-scatter.3
where the time goes:
time: 239 us; the launch traced here: 237 us
  other arithmetic  62.3 us (26%)
  blocking collectives  57.3 us (24%)
  local copies, waits for them, and re-layouts  53.5 us (22%)
  waiting for transfers between devices  31.6 us (13%)
  between operations  16.1 us (7%)
  matrix products  12.5 us (5%)
  starting transfers between devices  2.67 us (1%)
    convert_element_type x27, other arithmetic, add_panel(): jnp.cos(angle).astype(jnp.bfloat16)  58.4 us
    dynamic_slice x27, local copies, waits for them, and re-layouts, add_panel(): lax.dynamic_slice_in_dim(coefficients, offset, span_cols, 1)  46.9 us
    all_gather x1, blocking collectives, on_device(): all_points = lax.all_gather(local_points, ('ga', 'orb'), axis=1, tiled=True)  43.4 us
    reduce_scatter x1, waiting for transfers between devices, on_device(): lax.psum_scatter(phase_values(reordered, triples, coefficients), 'orb', s...  31.3 us
    unnamed x1, blocking collectives  13.9 us
    dot_general x27, matrix products, add_panel(): jnp.dot(phases, weights, preferred_element_type=jnp.float32)  12.5 us
  transfers between devices with their start and end apart: 2, of which 2 were waited for; matrix products, arithmetic and copies ran while one was open for 0% of the time, Pallas kernels for 0%

commit v1 on v0

v1 whole, which is shorter than its diff:
```python
import functools
import math

import jax
import jax.numpy as jnp
from jax import lax
from jax.experimental import pallas as pl
from jax.experimental.pallas import tpu as pltpu
from jax.sharding import PartitionSpec as P

MESH = pl.DeviceIdType.MESH
LANES = 128
SIN = (4.4409175764498094, -7.256811405668293, 3.2296557608294836)
COS = (1.4141797907346831, -6.976861782062955, 5.7090010941235345, -1.7141125404832036)
LAST = (((1,), (1,)), ((), ()))


def in_three(x):
    high = x.astype(jnp.bfloat16).astype(jnp.float32)
    rest = x - high
    middle = rest.astype(jnp.bfloat16).astype(jnp.float32)
    return high, middle, (rest - middle).astype(jnp.bfloat16).astype(jnp.float32)


def kernel(
    n_ga, n_orb, quad_count,
    coef, triples, elec, ions, assign, rot, quad, inv, out,
    held, held_sem, gathered, waves, spread, rows, phase_lhs, weight, angle, acc, total,
    outgoing, incoming, send_a, recv_a, send_b, recv_b,
):
    count = n_ga * n_orb
    me = lax.axis_index("ga") * n_orb + lax.axis_index("orb")
    chunks, _, span, columns = held.shape

    def coef_copy(c):
        return pltpu.make_async_copy(
            coef.at[:, pl.ds(c * span, span), :], held.at[c], held_sem.at[c]
        )

    def peer(i):
        other = lax.rem(me + i, count)
        return other, (other // n_orb, lax.rem(other, n_orb))

    barrier = pltpu.get_barrier_semaphore()

    def greet(i, carry):
        pl.semaphore_signal(barrier, inc=1, device_id=peer(i)[1], device_id_type=MESH)
        return carry

    lax.fori_loop(1, count, greet, 0)
    for c in range(chunks):
        coef_copy(c).start()

    lane = lax.broadcasted_iota(jnp.int32, ions.shape, 1)
    ion_row = jnp.sum(jnp.where(lane == assign[0], ions[...], 0.0), axis=1, keepdims=True)
    offset = elec[...] - ion_row
    radius = jnp.sqrt(jnp.sum(offset * offset, axis=0, keepdims=True))
    points = ion_row + radius * quad[rot[0]]
    points = points - jnp.round(points)
    gathered[me, :, pl.ds(0, columns)] = inv[...]
    gathered[me, :, pl.ds(columns, LANES)] = jnp.zeros((1, LANES), jnp.float32)
    for part, value in enumerate(in_three(points)):
        for d in range(3):
            first = columns + (part * 3 + d) * quad_count
            gathered[me, :, first : first + quad_count] = value[d : d + 1, :]

    pl.semaphore_wait(barrier, count - 1)

    def copy_a(slot, i):
        return pltpu.make_async_remote_copy(
            src_ref=gathered.at[me], dst_ref=gathered.at[slot],
            send_sem=send_a.at[i], recv_sem=recv_a.at[slot],
            device_id=peer(i)[1], device_id_type=MESH,
        )

    def send_rows(i, carry):
        copy_a(me, i).start()
        return carry

    lax.fori_loop(1, count, send_rows, 0)

    waves[...] = jnp.zeros_like(waves)
    waves[0:3, :] = triples[...].astype(jnp.float32)
    row = lax.broadcasted_iota(jnp.int32, (LANES, 16), 0)
    column = lax.broadcasted_iota(jnp.int32, (LANES, 16), 1)
    component = lax.rem(row // quad_count, 3)
    choose = jnp.where((component == column) & (row < 9 * quad_count), 1.0, 0.0)
    choose = choose.astype(jnp.bfloat16)
    for c in range(chunks):
        part = waves[:, c * span : (c + 1) * span].astype(jnp.bfloat16)
        spread[c] = jnp.dot(choose, part, preferred_element_type=jnp.float32).astype(jnp.bfloat16)
    acc[...] = jnp.zeros_like(acc)

    def receive_rows(i, carry):
        source = peer(i)[0]
        copy_a(source, i).wait_recv()
        return carry

    lax.fori_loop(1, count, receive_rows, 0)

    everything = gathered[...].reshape(count, columns + LANES)
    for part, value in enumerate(in_three(everything[:, :columns])):
        rows[part * count : (part + 1) * count, :] = value.astype(jnp.bfloat16)
    parts = everything[:, columns:]
    place = lax.rem(lax.broadcasted_iota(jnp.int32, parts.shape, 1), quad_count)
    for k in range(quad_count):
        mine = jnp.where(place == k, parts, 0.0).astype(jnp.bfloat16)
        phase_lhs[k * count : (k + 1) * count, :] = mine

    def one_chunk(c, carry):
        coef_copy(c).wait()
        for i in range(2):
            product = lax.dot_general(rows[...], held[c, i], LAST, preferred_element_type=jnp.float32)
            weight[i] = (product[:count] + product[count : 2 * count]) + product[2 * count :]
        angle[...] = jnp.dot(phase_lhs[...], spread[c], preferred_element_type=jnp.float32)
        for e in range(0, count, 8):
            w0 = weight[0, e : e + 8, :]
            w1 = weight[1, e : e + 8, :]
            acc[quad_count, e : e + 8, :] += fold(w0)
            for k in range(quad_count):
                turns = angle[k * count + e : k * count + e + 8, :]
                r = turns - jnp.round(turns)
                z = r * r
                sine = r * (SIN[0] + z * (SIN[1] + z * SIN[2]))
                cosine = COS[0] + z * (COS[1] + z * (COS[2] + z * COS[3]))
                acc[k, e : e + 8, :] += fold(sine * (w1 * cosine - w0 * sine))
        return carry

    lax.fori_loop(0, chunks, one_chunk, 0)

    place = lax.broadcasted_iota(jnp.int32, (count, LANES), 1)
    share = jnp.sum(acc[quad_count], axis=1, keepdims=True)
    share = jnp.broadcast_to(share, (count, LANES))
    for k in range(quad_count):
        share = share + jnp.where(place == k, jnp.sum(acc[k], axis=1, keepdims=True), 0.0)
    total[...] = share

    def copy_b(target, slot, i, device):
        return pltpu.make_async_remote_copy(
            src_ref=outgoing.at[target], dst_ref=incoming.at[slot],
            send_sem=send_b.at[i], recv_sem=recv_b.at[slot],
            device_id=device, device_id_type=MESH,
        )

    def send_share(i, carry):
        target, device = peer(i)
        outgoing[target] = total[pl.ds(target, 1), :]
        copy_b(target, me, i, device).start()
        return carry

    lax.fori_loop(1, count, send_share, 0)
    incoming[me] = total[pl.ds(me, 1), :]

    def receive_share(i, carry):
        source, device = peer(i)
        copy_b(source, source, i, device).wait_recv()
        return carry

    lax.fori_loop(1, count, receive_share, 0)
    out[...] = jnp.sum(incoming[...], axis=0)[:, :quad_count]

    def drain(i, carry):
        target, device = peer(i)
        copy_a(me, i).wait_send()
        copy_b(target, me, i, device).wait_send()
        return carry

    lax.fori_loop(1, count, drain, 0)


def fold(x):
    tiles = [x[:, j : j + LANES] for j in range(0, x.shape[1], LANES)]
    while len(tiles) > 1:
        pairs = [a + b for a, b in zip(tiles[0::2], tiles[1::2])]
        tiles = pairs + tiles[len(pairs) * 2 :]
    return tiles[0]


def on_device(mesh_shape, coef, triples, elec, ions, assign, rot, quad, inv):
    n_ga, n_orb = mesh_shape
    count = n_ga * n_orb
    quad_count = quad.shape[2]
    local, columns = coef.shape[1:]
    assert inv.shape[0] == 1 and 9 * quad_count <= LANES
    span = math.gcd(local, 1024)
    chunks = local // span
    smem = pl.BlockSpec(memory_space=pltpu.SMEM)
    vmem = pl.BlockSpec(memory_space=pltpu.VMEM)
    dma = pltpu.SemaphoreType.DMA
    return pl.pallas_call(
        functools.partial(kernel, n_ga, n_orb, quad_count),
        out_shape=jax.ShapeDtypeStruct((1, quad_count), jnp.float32),
        in_specs=[pl.BlockSpec(memory_space=pl.ANY), vmem, vmem, vmem, smem, smem, vmem, vmem],
        out_specs=vmem,
        scratch_shapes=[
            pltpu.VMEM((chunks, 2, span, columns), jnp.bfloat16),
            dma((chunks,)),
            pltpu.VMEM((count, 1, columns + LANES), jnp.float32),
            pltpu.VMEM((16, local), jnp.float32),
            pltpu.VMEM((chunks, LANES, span), jnp.bfloat16),
            pltpu.VMEM((3 * count, columns), jnp.bfloat16),
            pltpu.VMEM((quad_count * count, LANES), jnp.bfloat16),
            pltpu.VMEM((2, count, span), jnp.float32),
            pltpu.VMEM((quad_count * count, span), jnp.float32),
            pltpu.VMEM((quad_count + 1, count, LANES), jnp.float32),
            pltpu.VMEM((count, LANES), jnp.float32),
            pltpu.VMEM((count, 1, LANES), jnp.float32),
            pltpu.VMEM((count, 1, LANES), jnp.float32),
            dma((count,)),
            dma((count,)),
            dma((count,)),
            dma((count,)),
        ],
        compiler_params=pltpu.CompilerParams(
            collective_id=0, has_side_effects=True, vmem_limit_bytes=50 * 1024 * 1024
        ),
        name="ratios",
    )(coef, triples, elec, ions, assign, rot, quad, inv)


def solution(mesh):
    sizes = (mesh.shape["ga"], mesh.shape["orb"])
    return jax.shard_map(
        functools.partial(on_device, sizes),
        mesh=mesh,
        in_specs=(
            P(None, ("ga", "orb"), None),
            P(None, ("ga", "orb")),
            P(None, ("ga", "orb")),
            P(),
            P(("ga", "orb")),
            P(("ga", "orb")),
            P(),
            P(("ga", "orb"), None),
        ),
        out_specs=P(("ga", "orb"), None),
        check_vma=False,
    )
```

time: 239 us -> 40.2 us (0.17)
  other arithmetic: 62.3 us -> 0 us
  blocking collectives: 57.3 us -> 0 us
  local copies, waits for them, and re-layouts: 53.5 us -> 4.37 us
  Pallas kernels: 0 us -> 34.3 us
  waiting for transfers between devices: 31.6 us -> 0 us
  between operations: 16.1 us -> 1.32 us
  matrix products: 12.5 us -> 0 us
  starting transfers between devices: 2.67 us -> 0 us
    convert_element_type x27 -> x0, other arithmetic: 58.4 us -> none  [add_panel(): jnp.cos(angle).astype(jnp.bfloat16)]
    dynamic_slice x33 -> x0, local copies, waits for them, and re-layouts: 46.9 us -> none  [the longest x27 46.9 us: add_panel(): lax.dynamic_slice_in_dim(coefficients, offset, span_cols, 1)]
    all_gather x1 -> x0, blocking collectives: 43.4 us -> none  [on_device(): all_points = lax.all_gather(local_points, ('ga', 'orb'), axis=1, tiled=True)]
    pallas_call x0 -> x1, Pallas kernels: none -> 34.3 us  [on_device(): pl.pallas_call(functools.partial(kernel, n_ga, n_orb, quad_count), out_sh...]
    reduce_scatter x1 -> x0, waiting for transfers between devices: 31.3 us -> none  [on_device(): lax.psum_scatter(phase_values(reordered, triples, coefficients), 'orb', s...]
    unnamed x1 -> x0, blocking collectives: 13.9 us -> none
    dot_general x27 -> x0, matrix products: 12.5 us -> none  [add_panel(): jnp.dot(phases, weights, preferred_element_type=jnp.float32)]
    unnamed x9, local copies, waits for them, and re-layouts: 1.56 us -> 4.37 us
  transfers between devices with their start and end apart: 2 -> 0, of which waited for: 2 -> 0; matrix products, arithmetic and copies ran while one was open for 0% -> 0% of each run, Pallas kernels for 0% -> 0%
where the time goes in v1:
time: 40.2 us; the launch traced here: 40 us
  Pallas kernels  34.3 us (85%)
  local copies, waits for them, and re-layouts  4.37 us (11%)
  between operations  1.32 us (3%)
    pallas_call x1, Pallas kernels, on_device(): pl.pallas_call(functools.partial(kernel, n_ga, n_orb, quad_count), out_sh...  34.3 us
    unnamed x9, local copies, waits for them, and re-layouts  4.37 us

profile of v1, /device:TPU:0, one launch (start us, length us, event | category | flops | bytes accessed | tf_op | source)
XLA Modules:
  0.0 40.0 jit_solution(8266734532640945653)
XLA Ops:
  1.3 0.7 %copy.9.elec = f32[3,1]{1,0:T(4,128)S(1)} copy(f32[3,1]{0,1:T(1,128)} %param.10) | data formatting | bytes 24 | tf_op args[2]
  2.0 0.9 %copy.10.quad = f32[64,3,12]{2,1,0:T(4,128)S(1)} copy(f32[64,3,12]{0,2,1:T(8,128)} %param.14) | data formatting | bytes 18432 | tf_op args[6]
  2.9 0.0 copy-start
  2.9 0.9 %copy-done = s32[3,9216]{1,0:T(4,128)S(1)} copy-done((s32[3,9216]{1,0:T(4,128)S(1)}, s32[3,9216]{1,0:T(4,128)}, u32[]{:S(2)}) %copy-start) | copy-done | bytes 110616
  3.8 0.0 copy-start.1
  3.8 0.7 %copy-done.1 = f32[3,128]{1,0:T(4,128)S(1)} copy-done((f32[3,128]{1,0:T(4,128)S(1)}, f32[3,128]{1,0:T(4,128)}, u32[]{:S(2)}) %copy-start.1) | copy-done | bytes 1560
  4.5 0.0 copy-start.2
  4.5 0.7 %copy-done.2 = f32[1,512]{1,0:T(1,128)S(1)} copy-done((f32[1,512]{1,0:T(1,128)S(1)}, f32[1,512]{1,0:T(1,128)}, u32[]{:S(2)}) %copy-start.2) | copy-done | bytes 2072
  5.2 34.3 %ratios.1 = f32[1,12]{1,0:T(1,128)S(1)} custom-call(bf16[2,9216,512]{2,1,0:T(8,128)(2,1)} %coef.1, s32[3,9216]{1,0:T(4,128)S(1)} %copy-done, f32[3,1]{1,0:T(4,128)S(1)} %copy.9.elec, f32[3,128]{1,0:T(4,128)S(1)} %copy-done.1, s32[1]{0:T(128)S(6)} %copy.12.assign, s32[1]{0:T(128)S(6)} %copy.13.rot, f32[64,3,12]{2,1,0:T(4,128)S(1)} %copy.10.quad, ...), custom_call_target="tpu_custom_call" | custom-call | tf_op jit(solution)/shard_map/ratios/pallas_call | solution.py:190
  39.4 0.5 %copy.14 = f32[1,12]{1,0:T(1,128)} copy(f32[1,12]{1,0:T(1,128)S(1)} %ratios.1) | data formatting | bytes 96
Async XLA Ops:
  2.9 0.9 %copy-start = (s32[3,9216]{1,0:T(4,128)S(1)}, s32[3,9216]{1,0:T(4,128)}, u32[]{:S(2)}) copy-start(s32[3,9216]{1,0:T(4,128)} %triples.1) | copy-start | bytes 331780
  3.8 0.7 %copy-start.1 = (f32[3,128]{1,0:T(4,128)S(1)}, f32[3,128]{1,0:T(4,128)}, u32[]{:S(2)}) copy-start(f32[3,128]{1,0:T(4,128)} %ions.1) | copy-start | bytes 4612
  4.5 0.7 %copy-start.2 = (f32[1,512]{1,0:T(1,128)S(1)}, f32[1,512]{1,0:T(1,128)}, u32[]{:S(2)}) copy-start(f32[1,512]{1,0:T(1,128)} %inv.1) | copy-start | bytes 6148

commit v2 on v1

v2 whole, which is shorter than its diff:
```python
import functools
import math

import jax
import jax.numpy as jnp
from jax import lax
from jax.experimental import pallas as pl
from jax.experimental.pallas import tpu as pltpu
from jax.sharding import PartitionSpec as P

MESH = pl.DeviceIdType.MESH
LANES = 128
SIN = (4.4409175764498094, -7.256811405668293, 3.2296557608294836)
COS = (1.4141797907346831, -6.976861782062955, 5.7090010941235345, -1.7141125404832036)
LAST = (((1,), (1,)), ((), ()))


ROUNDER = 1.5 * 2.0**23


def in_three(x):
    high = x.astype(jnp.bfloat16).astype(jnp.float32)
    rest = x - high
    middle = rest.astype(jnp.bfloat16).astype(jnp.float32)
    return high, middle, (rest - middle).astype(jnp.bfloat16).astype(jnp.float32)


def rounded(x):
    return (x + ROUNDER) - ROUNDER


def each_peer(count, step):
    if count <= 32:
        for i in range(1, count):
            step(i)
    else:

        def body(i, carry):
            step(i)
            return carry

        lax.fori_loop(1, count, body, 0)


def kernel(
    n_ga, n_orb, quad_count,
    coef, triples_in, elec_in, ions_in, assign, rot, quad_in, inv_in, out,
    held, held_sem, triples, elec, ions, quad, inv, small_sem,
    gathered, waves, spread, rows, phase_lhs, weight_a, angle_a, weight_b, angle_b, acc,
    outgoing, incoming, send_a, recv_a, send_b, recv_b,
):
    count = n_ga * n_orb
    me = lax.axis_index("ga") * n_orb + lax.axis_index("orb")
    chunks, _, span, columns = held.shape

    def coef_copy(c):
        return pltpu.make_async_copy(
            coef.at[:, pl.ds(c * span, span), :], held.at[c], held_sem.at[c]
        )

    def peer(i):
        other = lax.rem(me + i, count)
        return other, (other // n_orb, lax.rem(other, n_orb))

    small = [
        pltpu.make_async_copy(src, dst, small_sem.at[i])
        for i, (src, dst) in enumerate(
            [(ions_in, ions), (elec_in, elec), (quad_in, quad), (inv_in, inv), (triples_in, triples)]
        )
    ]
    for copy in small:
        copy.start()
    barrier = pltpu.get_barrier_semaphore()

    def greet(i):
        pl.semaphore_signal(barrier, inc=1, device_id=peer(i)[1], device_id_type=MESH)

    each_peer(count, greet)
    for c in range(chunks):
        coef_copy(c).start()
    for copy in small:
        copy.wait()

    lane = lax.broadcasted_iota(jnp.int32, ions.shape, 1)
    ion = jnp.sum(jnp.where(lane == assign[0], ions[...], 0.0), axis=1, keepdims=True)
    square = None
    for d in range(3):
        offset = elec[0:1, d : d + 1] - ion[d : d + 1, :]
        square = offset * offset if square is None else square + offset * offset
    radius = jnp.sqrt(square)
    lane = lax.broadcasted_iota(jnp.int32, (quad_count, LANES), 1)
    within = lax.rem(lane, 3 * quad_count)
    k_of = lax.broadcasted_iota(jnp.int32, (quad_count, LANES), 0)
    chosen = lax.broadcasted_iota(jnp.int32, quad.shape[1:], 1) == rot[0]
    points = jnp.zeros((quad_count, LANES), jnp.float32)
    for d in range(3):
        move = jnp.sum(jnp.where(chosen, quad[d], 0.0), axis=1, keepdims=True)
        located = ion[d : d + 1, :] + radius * move
        points = points + jnp.where(within == d * quad_count + k_of, located, 0.0)
    points = jnp.sum(points, axis=0, keepdims=True)
    high, middle, low = in_three(points - rounded(points))
    lane = lax.broadcasted_iota(jnp.int32, (1, LANES), 1)
    size = 3 * quad_count
    parts = jnp.where(lane < size, high, jnp.where(lane < 2 * size, middle, low))
    gathered[me, :, pl.ds(0, columns)] = inv[...]
    gathered[me, :, pl.ds(columns, LANES)] = jnp.where(lane < 3 * size, parts, 0.0)

    waves[...] = jnp.zeros_like(waves)
    waves[0:3, :] = triples[...].astype(jnp.float32)
    row = lax.broadcasted_iota(jnp.int32, (LANES, 16), 0)
    column = lax.broadcasted_iota(jnp.int32, (LANES, 16), 1)
    component = lax.rem(row // quad_count, 3)
    choose = jnp.where((component == column) & (row < 9 * quad_count), 1.0, 0.0)
    choose = choose.astype(jnp.bfloat16)
    for c in range(chunks):
        part = waves[:, c * span : (c + 1) * span].astype(jnp.bfloat16)
        spread[c] = jnp.dot(choose, part, preferred_element_type=jnp.float32).astype(jnp.bfloat16)
    acc[...] = jnp.zeros_like(acc)

    pl.semaphore_wait(barrier, count - 1)

    def send_row(i):
        pltpu.make_async_remote_copy(
            src_ref=gathered.at[me], dst_ref=gathered.at[me],
            send_sem=send_a, recv_sem=recv_a,
            device_id=peer(i)[1], device_id_type=MESH,
        ).start()

    each_peer(count, send_row)

    def wait_others(buffer, sem):
        others = buffer.at[pl.ds(0, count - 1)]
        pltpu.make_async_copy(others, others, sem).wait()

    wait_others(gathered, recv_a)

    everything = gathered[...].reshape(count, columns + LANES)
    for part, value in enumerate(in_three(everything[:, :columns])[:2]):
        rows[part * count : (part + 1) * count, :] = value.astype(jnp.bfloat16)
    parts = everything[:, columns:]
    place = lax.rem(lax.broadcasted_iota(jnp.int32, parts.shape, 1), quad_count)
    for k in range(quad_count):
        mine = jnp.where(place == k, parts, 0.0).astype(jnp.bfloat16)
        phase_lhs[k * count : (k + 1) * count, :] = mine

    width = math.gcd(span, 256)
    pieces = span // width
    tiles = count // 8

    def produce(c, weight, angle, piece):
        cols = slice(piece * width, (piece + 1) * width)
        for i in range(2):
            product = lax.dot_general(
                rows[...], held[c, i, cols, :], LAST, preferred_element_type=jnp.float32
            )
            weight[i, :, cols] = product[:count] + product[count:]
        angle[:, cols] = jnp.dot(
            phase_lhs[...], spread[c, :, cols], preferred_element_type=jnp.float32
        )

    def consume(weight, angle, tile):
        e = tile * 8
        w0 = weight[0, e : e + 8, :]
        w1 = weight[1, e : e + 8, :]
        acc[quad_count, e : e + 8, :] += fold(w0)
        for k in range(quad_count):
            turns = angle[k * count + e : k * count + e + 8, :]
            r = turns - rounded(turns)
            z = r * r
            sine = r * (SIN[0] + z * (SIN[1] + z * SIN[2]))
            cosine = COS[0] + z * (COS[1] + z * (COS[2] + z * COS[3]))
            acc[k, e : e + 8, :] += fold(sine * (w1 * cosine - w0 * sine))

    def both(now, c, later):
        coef_copy(c).wait()
        for tile in range(tiles):
            for piece in range(tile * pieces // tiles, (tile + 1) * pieces // tiles):
                produce(c, *later, piece)
            consume(*now, tile)

    even, odd = (weight_a, angle_a), (weight_b, angle_b)
    coef_copy(0).wait()
    for piece in range(pieces):
        produce(0, *even, piece)

    def two_chunks(i, carry):
        both(even, 2 * i + 1, odd)
        both(odd, 2 * i + 2, even)
        return carry

    lax.fori_loop(0, (chunks - 1) // 2, two_chunks, 0)
    last = even
    if chunks % 2 == 0:
        both(even, chunks - 1, odd)
        last = odd
    for tile in range(tiles):
        consume(*last, tile)

    place = lax.broadcasted_iota(jnp.int32, (count, LANES), 1)
    share = jnp.sum(acc[quad_count], axis=1, keepdims=True)
    share = jnp.broadcast_to(share, (count, LANES))
    for k in range(quad_count):
        share = share + jnp.where(place == k, jnp.sum(acc[k], axis=1, keepdims=True), 0.0)
    outgoing[...] = share.reshape(count, 1, LANES)

    def send_share(i):
        target, device = peer(i)
        pltpu.make_async_remote_copy(
            src_ref=outgoing.at[target], dst_ref=incoming.at[me],
            send_sem=send_b, recv_sem=recv_b,
            device_id=device, device_id_type=MESH,
        ).start()

    each_peer(count, send_share)
    incoming[me] = outgoing[me]
    wait_others(gathered, send_a)
    wait_others(incoming, recv_b)
    out[...] = jnp.sum(incoming[...], axis=0)[:, :quad_count]
    wait_others(outgoing, send_b)


def fold(x):
    tiles = [x[:, j : j + LANES] for j in range(0, x.shape[1], LANES)]
    while len(tiles) > 1:
        pairs = [a + b for a, b in zip(tiles[0::2], tiles[1::2])]
        tiles = pairs + tiles[len(pairs) * 2 :]
    return tiles[0]


def on_device(mesh_shape, coef, triples, elec, ions, assign, rot, quad, inv):
    n_ga, n_orb = mesh_shape
    count = n_ga * n_orb
    quad_count = quad.shape[2]
    local, columns = coef.shape[1:]
    assert inv.shape[0] == 1 and 9 * quad_count <= LANES
    span = math.gcd(local, 1024)
    chunks = local // span
    smem = pl.BlockSpec(memory_space=pltpu.SMEM)
    hbm = pl.BlockSpec(memory_space=pltpu.HBM)
    dma = pltpu.SemaphoreType.DMA
    elec = elec.T
    quad = jnp.transpose(quad, (1, 2, 0))
    weight = pltpu.VMEM((2, count, span), jnp.float32)
    angle = pltpu.VMEM((quad_count * count, span), jnp.float32)
    return pl.pallas_call(
        functools.partial(kernel, n_ga, n_orb, quad_count),
        out_shape=jax.ShapeDtypeStruct((1, quad_count), jnp.float32),
        in_specs=[hbm, hbm, hbm, hbm, smem, smem, hbm, hbm],
        out_specs=pl.BlockSpec(memory_space=pltpu.VMEM),
        scratch_shapes=[
            pltpu.VMEM((chunks, 2, span, columns), jnp.bfloat16),
            dma((chunks,)),
            pltpu.VMEM(triples.shape, jnp.int32),
            pltpu.VMEM(elec.shape, jnp.float32),
            pltpu.VMEM(ions.shape, jnp.float32),
            pltpu.VMEM(quad.shape, jnp.float32),
            pltpu.VMEM(inv.shape, jnp.float32),
            dma((5,)),
            pltpu.VMEM((count, 1, columns + LANES), jnp.float32),
            pltpu.VMEM((16, local), jnp.float32),
            pltpu.VMEM((chunks, LANES, span), jnp.bfloat16),
            pltpu.VMEM((2 * count, columns), jnp.bfloat16),
            pltpu.VMEM((quad_count * count, LANES), jnp.bfloat16),
            weight,
            angle,
            weight,
            angle,
            pltpu.VMEM((quad_count + 1, count, LANES), jnp.float32),
            pltpu.VMEM((count, 1, LANES), jnp.float32),
            pltpu.VMEM((count, 1, LANES), jnp.float32),
            dma,
            dma,
            dma,
            dma,
        ],
        compiler_params=pltpu.CompilerParams(
            collective_id=0, has_side_effects=True, vmem_limit_bytes=60 * 1024 * 1024
        ),
        name="ratios",
    )(coef, triples, elec, ions, assign, rot, quad, inv)


def solution(mesh):
    sizes = (mesh.shape["ga"], mesh.shape["orb"])
    return jax.shard_map(
        functools.partial(on_device, sizes),
        mesh=mesh,
        in_specs=(
            P(None, ("ga", "orb"), None),
            P(None, ("ga", "orb")),
            P(None, ("ga", "orb")),
            P(),
            P(("ga", "orb")),
            P(("ga", "orb")),
            P(),
            P(("ga", "orb"), None),
        ),
        out_specs=P(("ga", "orb"), None),
        check_vma=False,
    )
```

time: 40.2 us -> 33.8 us (0.84)
  Pallas kernels: 34.3 us -> 31.1 us
  local copies, waits for them, and re-layouts: 4.37 us -> 1.19 us
    unnamed x9 -> x1, local copies, waits for them, and re-layouts: 4.37 us -> 1.19 us
    pallas_call x1, Pallas kernels: 34.3 us -> 31.1 us  [on_device(): pl.pallas_call(functools.partial(kernel, n_ga, n_orb, quad_count), out_sh...]
where the time goes in v2:
time: 33.8 us; the launch traced here: 33.6 us
  Pallas kernels  31.1 us (92%)
  between operations  1.3 us (4%)
  local copies, waits for them, and re-layouts  1.19 us (4%)
    pallas_call x1, Pallas kernels, on_device(): pl.pallas_call(functools.partial(kernel, n_ga, n_orb, quad_count), out_sh...  31.1 us
    unnamed x1, local copies, waits for them, and re-layouts  1.19 us

profile of v2, /device:TPU:0, one launch (start us, length us, event | category | flops | bytes accessed | tf_op | source)
XLA Modules:
  0.0 33.6 jit_solution(12329234681558120417)
XLA Ops:
  1.3 31.1 %ratios.1 = f32[1,12]{1,0:T(1,128)} custom-call(bf16[2,9216,512]{2,1,0:T(8,128)(2,1)} %coef.1, s32[3,9216]{1,0:T(4,128)} %triples_in.1, f32[1,3]{1,0:T(1,128)} %bitcast.3, f32[3,128]{1,0:T(4,128)} %ions_in.1, s32[1]{0:T(128)S(6)} %copy.10.assign, s32[1]{0:T(128)S(6)} %copy.11.rot, f32[3,12,64]{2,1,0:T(8,128)} %bitcast.2, f32[1,512]{1,0:T(1,128)} %inv_in.1), custom_call_target="tpu_custom_call" | custom-call | tf_op jit(solution)/shard_map/ratios/pallas_call | solution.py:245
  32.4 1.2 %copy.12 = f32[1,12]{1,0:T(1,128)} copy(f32[1,12]{1,0:T(1,128)} %ratios.1) | data formatting | bytes 96

commit v3 on v2

--- a/solution.py
+++ b/solution.py
@@ -78,7 +78,7 @@
     each_peer(count, greet)
     for c in range(chunks):
         coef_copy(c).start()
-    for copy in small:
+    for copy in small[:-1]:
         copy.wait()
 
     lane = lax.broadcasted_iota(jnp.int32, ions.shape, 1)
@@ -105,6 +105,18 @@
     gathered[me, :, pl.ds(0, columns)] = inv[...]
     gathered[me, :, pl.ds(columns, LANES)] = jnp.where(lane < 3 * size, parts, 0.0)
 
+    pl.semaphore_wait(barrier, count - 1)
+
+    def send_row(i):
+        pltpu.make_async_remote_copy(
+            src_ref=gathered.at[me], dst_ref=gathered.at[me],
+            send_sem=send_a, recv_sem=recv_a,
+            device_id=peer(i)[1], device_id_type=MESH,
+        ).start()
+
+    each_peer(count, send_row)
+
+    small[-1].wait()
     waves[...] = jnp.zeros_like(waves)
     waves[0:3, :] = triples[...].astype(jnp.float32)
     row = lax.broadcasted_iota(jnp.int32, (LANES, 16), 0)
@@ -116,17 +128,6 @@
         part = waves[:, c * span : (c + 1) * span].astype(jnp.bfloat16)
         spread[c] = jnp.dot(choose, part, preferred_element_type=jnp.float32).astype(jnp.bfloat16)
     acc[...] = jnp.zeros_like(acc)
-
-    pl.semaphore_wait(barrier, count - 1)
-
-    def send_row(i):
-        pltpu.make_async_remote_copy(
-            src_ref=gathered.at[me], dst_ref=gathered.at[me],
-            send_sem=send_a, recv_sem=recv_a,
-            device_id=peer(i)[1], device_id_type=MESH,
-        ).start()
-
-    each_peer(count, send_row)
 
     def wait_others(buffer, sem):
         others = buffer.at[pl.ds(0, count - 1)]
@@ -244,7 +245,7 @@
     angle = pltpu.VMEM((quad_count * count, span), jnp.float32)
     return pl.pallas_call(
         functools.partial(kernel, n_ga, n_orb, quad_count),
-        out_shape=jax.ShapeDtypeStruct((1, quad_count), jnp.float32),
+        out_shape=pltpu.VMEM((1, quad_count), jnp.float32),
         in_specs=[hbm, hbm, hbm, hbm, smem, smem, hbm, hbm],
         out_specs=pl.BlockSpec(memory_space=pltpu.VMEM),
         scratch_shapes=[

time: 33.8 us -> 32.5 us (0.962)
  local copies, waits for them, and re-layouts: 1.19 us -> 0.51 us
  Pallas kernels: 31.1 us -> 30.5 us
    unnamed x1, local copies, waits for them, and re-layouts: 1.19 us -> 0.51 us
    pallas_call x1, Pallas kernels: 31.1 us -> 30.5 us  [on_device(): pl.pallas_call(functools.partial(kernel, n_ga, n_orb, quad_count), out_sh...]
where the time goes in v3:
time: 32.5 us; the launch traced here: 32.3 us
  Pallas kernels  30.5 us (94%)
  between operations  1.3 us (4%)
  local copies, waits for them, and re-layouts  0.51 us (2%)
    pallas_call x1, Pallas kernels, on_device(): pl.pallas_call(functools.partial(kernel, n_ga, n_orb, quad_count), out_sh...  30.5 us

profile of v3, /device:TPU:0, one launch (start us, length us, event | category | flops | bytes accessed | tf_op | source)
XLA Modules:
  0.0 32.3 jit_solution(5694932368860390245)
XLA Ops:
  1.3 30.5 %ratios.1 = f32[1,12]{1,0:T(1,128)S(1)} custom-call(bf16[2,9216,512]{2,1,0:T(8,128)(2,1)} %coef.1, s32[3,9216]{1,0:T(4,128)} %triples_in.1, f32[1,3]{1,0:T(1,128)} %bitcast.3, f32[3,128]{1,0:T(4,128)} %ions_in.1, s32[1]{0:T(128)S(6)} %copy.11.assign, s32[1]{0:T(128)S(6)} %copy.12.rot, f32[3,12,64]{2,1,0:T(8,128)} %bitcast.2, f32[1,512]{1,0:T(1,128)} %inv_in.1), custom_call_target="tpu_custom_call" | custom-call | tf_op jit(solution)/shard_map/ratios/pallas_call | solution.py:246
  31.8 0.5 %copy.10 = f32[1,12]{1,0:T(1,128)} copy(f32[1,12]{1,0:T(1,128)S(1)} %ratios.1) | data formatting | bytes 96

commit v4 on v3

--- a/solution.py
+++ b/solution.py
@@ -10,8 +10,11 @@
 
 MESH = pl.DeviceIdType.MESH
 LANES = 128
-SIN = (4.4409175764498094, -7.256811405668293, 3.2296557608294836)
-COS = (1.4141797907346831, -6.976861782062955, 5.7090010941235345, -1.7141125404832036)
+SIN = (6.281280240499966, -41.09525634382307, 73.58572901915015)
+ATAN = (
+    0.15913366845101437, -0.052569633937468316, 0.02867321820152353,
+    -0.01355301556095631, 0.003317582793410697,
+)
 LAST = (((1,), (1,)), ((), ()))
 
 
@@ -27,6 +30,20 @@
 
 def rounded(x):
     return (x + ROUNDER) - ROUNDER
+
+
+def polar(x, y):
+    across, along = jnp.abs(y), jnp.abs(x)
+    largest = jnp.maximum(across, along)
+    q = jnp.minimum(across, along) / jnp.maximum(largest, 1e-37)
+    z = q * q
+    turns = ATAN[4]
+    for term in ATAN[3::-1]:
+        turns = term + z * turns
+    turns = q * turns
+    turns = jnp.where(across > along, 0.25 - turns, turns)
+    turns = jnp.where(x < 0, 0.5 - turns, turns)
+    return largest * jnp.sqrt(1.0 + z), jnp.where(y < 0, -turns, turns)
 
 
 def each_peer(count, step):
@@ -150,27 +167,26 @@
 
     def produce(c, weight, angle, piece):
         cols = slice(piece * width, (piece + 1) * width)
+        w = []
         for i in range(2):
             product = lax.dot_general(
                 rows[...], held[c, i, cols, :], LAST, preferred_element_type=jnp.float32
             )
-            weight[i, :, cols] = product[:count] + product[count:]
+            w.append(product[:count] + product[count:])
+        weight[0, :, cols], weight[1, :, cols] = polar(*w)
         angle[:, cols] = jnp.dot(
             phase_lhs[...], spread[c, :, cols], preferred_element_type=jnp.float32
         )
 
     def consume(weight, angle, tile):
         e = tile * 8
-        w0 = weight[0, e : e + 8, :]
-        w1 = weight[1, e : e + 8, :]
-        acc[quad_count, e : e + 8, :] += fold(w0)
+        size = weight[0, e : e + 8, :]
+        shift = weight[1, e : e + 8, :]
         for k in range(quad_count):
-            turns = angle[k * count + e : k * count + e + 8, :]
-            r = turns - rounded(turns)
-            z = r * r
-            sine = r * (SIN[0] + z * (SIN[1] + z * SIN[2]))
-            cosine = COS[0] + z * (COS[1] + z * (COS[2] + z * COS[3]))
-            acc[k, e : e + 8, :] += fold(sine * (w1 * cosine - w0 * sine))
+            turns = angle[k * count + e : k * count + e + 8, :] - shift
+            v = 0.25 - jnp.abs(turns - rounded(turns))
+            z = v * v
+            acc[k, e : e + 8, :] += fold((size * v) * (SIN[0] + z * (SIN[1] + z * SIN[2])))
 
     def both(now, c, later):
         coef_copy(c).wait()
@@ -198,8 +214,7 @@
         consume(*last, tile)
 
     place = lax.broadcasted_iota(jnp.int32, (count, LANES), 1)
-    share = jnp.sum(acc[quad_count], axis=1, keepdims=True)
-    share = jnp.broadcast_to(share, (count, LANES))
+    share = jnp.zeros((count, LANES), jnp.float32)
     for k in range(quad_count):
         share = share + jnp.where(place == k, jnp.sum(acc[k], axis=1, keepdims=True), 0.0)
     outgoing[...] = share.reshape(count, 1, LANES)
@@ -266,7 +281,7 @@
             angle,
             weight,
             angle,
-            pltpu.VMEM((quad_count + 1, count, LANES), jnp.float32),
+            pltpu.VMEM((quad_count, count, LANES), jnp.float32),
             pltpu.VMEM((count, 1, LANES), jnp.float32),
             pltpu.VMEM((count, 1, LANES), jnp.float32),
             dma,

time: 32.5 us -> 32.1 us (0.988)
  Pallas kernels: 30.5 us -> 30.1 us
    pallas_call x1, Pallas kernels: 30.5 us -> 30.1 us  [on_device(): pl.pallas_call(functools.partial(kernel, n_ga, n_orb, quad_count), out_sh...]
where the time goes in v4:
time: 32.1 us; the launch traced here: 31.9 us
  Pallas kernels  30.1 us (94%)
  between operations  1.3 us (4%)
  local copies, waits for them, and re-layouts  0.51 us (2%)
    pallas_call x1, Pallas kernels, on_device(): pl.pallas_call(functools.partial(kernel, n_ga, n_orb, quad_count), out_sh...  30.1 us

profile of v4, /device:TPU:0, one launch (start us, length us, event | category | flops | bytes accessed | tf_op | source)
XLA Modules:
  0.0 31.9 jit_solution(16260014046436618718)
XLA Ops:
  1.3 30.1 %ratios.1 = f32[1,12]{1,0:T(1,128)S(1)} custom-call(bf16[2,9216,512]{2,1,0:T(8,128)(2,1)} %coef.1, s32[3,9216]{1,0:T(4,128)} %triples_in.1, f32[1,3]{1,0:T(1,128)} %bitcast.3, f32[3,128]{1,0:T(4,128)} %ions_in.1, s32[1]{0:T(128)S(6)} %copy.11.assign, s32[1]{0:T(128)S(6)} %copy.12.rot, f32[3,12,64]{2,1,0:T(8,128)} %bitcast.2, f32[1,512]{1,0:T(1,128)} %inv_in.1), custom_call_target="tpu_custom_call" | custom-call | tf_op jit(solution)/shard_map/ratios/pallas_call | solution.py:261
  31.4 0.5 %copy.10 = f32[1,12]{1,0:T(1,128)} copy(f32[1,12]{1,0:T(1,128)S(1)} %ratios.1) | data formatting | bytes 96
